TPU v7x, 128 devices: a whole 4x4x4 slice. The times are simulated.
128 devices in a mesh: wide: 16 (over y, x_hi, core), narrow: 8 (over x_lo, z).
Axes of the slice: x: 4 (x_hi: 2, x_lo: 2; x = x_hi * 2 + x_lo), y: 4, z: 4, core: 2. Of those that a mesh axis runs over, the one named last changes fastest.
Arguments:
- layer_input: bfloat16 [512, 18432], P('wide'), may hold values from -4 to 4
- norm_gain: float32 [18432], replicated, may hold values from 0.1 to 1.9
- w_query: bfloat16 [18432, 12288], P('narrow', 'wide'), may hold values from -0.125 to 0.125
- w_keyvalue: bfloat16 [18432, 512], P('narrow', 'wide'), may hold values from -0.046875 to 0.046875
- w_gate: bfloat16 [18432, 36864], P('narrow', 'wide'), may hold values from -0.046875 to 0.046875
- w_up: bfloat16 [18432, 36864], P('narrow', 'wide'), may hold values from -0.046875 to 0.046875
- key_cache: bfloat16 [512, 512, 256], P(('wide', 'narrow')), may hold values from -6 to 6
- value_cache: bfloat16 [512, 512, 256], P(('wide', 'narrow')), may hold values from -6 to 6
- cache_lengths: int32 [512], P(('wide', 'narrow')), may hold values from 1 to 512, as said below
Outputs:
- attended_heads: bfloat16 [512, 12288], P(None, ('wide', 'narrow'))
- hidden_units: bfloat16 [512, 36864], P(None, ('wide', 'narrow'))
Inputs may be any that keep to these rules, and one draw needn't show every extreme that they name: `cache_lengths`: some row has all 512 positions filled and some row has one.
All inputs are finite; a program needn't handle non-finite values.
Results may differ from a plain program's by a relative error of at most 0.0097.
Values may be sent and summed in bfloat16 or wider, within the bound.
A program may use at most 128 MiB of HBM per device.

v0:
```python
import jax
import jax.numpy as jnp
from jax import lax
from jax.sharding import PartitionSpec as P


def row_attention(query, keyvalue, keys, values, length):
    head_dim = keys.shape[1]
    scale = head_dim ** (-0.5)
    heads = query.reshape(-1, head_dim)
    scores = jnp.dot(heads, keys.T, preferred_element_type=jnp.float32) * scale
    valid = jnp.arange(keys.shape[0], dtype=jnp.int32) < length
    raised = jnp.where(valid[None, :], jnp.exp(scores), 0.0)
    own_score = jnp.dot(heads, keyvalue[:head_dim], preferred_element_type=jnp.float32) * scale
    own_weight = jnp.exp(own_score)
    total = jnp.sum(raised, axis=1) + own_weight
    probs = (raised / total[:, None]).astype(jnp.bfloat16)
    own_prob = (own_weight / total).astype(jnp.bfloat16)
    attended = jnp.dot(probs, values, preferred_element_type=jnp.float32)
    attended = (
        attended
        + own_prob.astype(jnp.float32)[:, None] * keyvalue[head_dim:].astype(jnp.float32)[None, :]
    )
    return attended.astype(jnp.bfloat16).reshape(-1)


def layer_norm(rows, norm_gain):
    values = rows.astype(jnp.float32)
    average = jnp.mean(values, axis=1, keepdims=True)
    centred = values - average
    spread = jnp.mean(centred * centred, axis=1, keepdims=True)
    return (centred * lax.rsqrt(spread + 1e-05) * norm_gain[None, :]).astype(jnp.bfloat16)


def narrow_major(array, n_wide, n_narrow, rows_dev):
    columns = array.shape[1]
    blocks = array.reshape(n_wide, n_narrow, rows_dev, columns).transpose(1, 0, 2, 3)
    return blocks.reshape(n_wide * n_narrow * rows_dev, columns)


def body(
    layer_input, norm_gain, w_query, w_keyvalue, w_gate, w_up, key_cache, value_cache, cache_lengths
):
    n_wide = lax.axis_size("wide")
    n_narrow = lax.axis_size("narrow")
    narrow_index = lax.axis_index("narrow")
    rows_dev = key_cache.shape[0]
    feature_slab = w_query.shape[0]
    query_cols = w_query.shape[1]
    pair_cols = w_keyvalue.shape[1]
    unit_cols = w_gate.shape[1]
    normed = layer_norm(layer_input, norm_gain)
    normed_part = lax.dynamic_slice_in_dim(normed, narrow_index * feature_slab, feature_slab, 1)
    piece = lax.all_gather(normed_part, "wide", axis=0, tiled=True)
    partial_value = jnp.concatenate(
        [
            jnp.dot(piece, w_query, preferred_element_type=jnp.float32),
            jnp.dot(piece, w_keyvalue, preferred_element_type=jnp.float32),
            jnp.dot(piece, w_gate, preferred_element_type=jnp.float32),
            jnp.dot(piece, w_up, preferred_element_type=jnp.float32),
        ],
        axis=1,
    )
    query_part = partial_value[:, :query_cols]
    pair_part = partial_value[:, query_cols : query_cols + pair_cols]
    gate_part = partial_value[:, query_cols + pair_cols : query_cols + pair_cols + unit_cols]
    upper_part = partial_value[:, query_cols + pair_cols + unit_cols :]
    query_sum, pair_sum, gate_sum, upper_sum = (
        lax.psum_scatter(
            narrow_major(query_part, n_wide, n_narrow, rows_dev),
            "narrow",
            scatter_dimension=0,
            tiled=True,
        ),
        lax.psum_scatter(
            narrow_major(pair_part, n_wide, n_narrow, rows_dev),
            "narrow",
            scatter_dimension=0,
            tiled=True,
        ),
        lax.psum_scatter(gate_part, "narrow", scatter_dimension=1, tiled=True),
        lax.psum_scatter(upper_part, "narrow", scatter_dimension=1, tiled=True),
    )
    hidden = (jax.nn.silu(gate_sum) * upper_sum).astype(jnp.bfloat16)
    query_rows, pair_rows = (
        lax.all_to_all(
            query_sum.astype(jnp.bfloat16), "wide", split_axis=0, concat_axis=1, tiled=True
        ),
        lax.all_to_all(
            pair_sum.astype(jnp.bfloat16), "wide", split_axis=0, concat_axis=1, tiled=True
        ),
    )
    attended = jax.vmap(row_attention)(query_rows, pair_rows, key_cache, value_cache, cache_lengths)
    attended_cols = lax.all_to_all(
        attended, ("wide", "narrow"), split_axis=1, concat_axis=0, tiled=True
    )
    return (attended_cols, hidden)


def solution(mesh):
    placed = (
        P("wide", None),
        P(),
        P("narrow", "wide"),
        P("narrow", "wide"),
        P("narrow", "wide"),
        P("narrow", "wide"),
        P(("wide", "narrow"), None, None),
        P(("wide", "narrow"), None, None),
        P(("wide", "narrow")),
    )
    return jax.shard_map(
        body,
        mesh=mesh,
        in_specs=placed,
        out_specs=(P(None, ("wide", "narrow")), P(None, ("wide", "narrow"))),
        check_vma=False,
    )
```

profile of v0, /device:TPU:1, one launch (start us, length us, event | category | flops | bytes accessed | tf_op | source)
XLA Modules:
  0.0 277.5 jit_solution(5520436019102063758)
XLA Ops:
  7.2 0.0 all-gather.2.cloned.1.call-start
  7.2 1.7 convert_reduce_fusion
  8.9 3.2 %multiply_reduce_fusion = (f32[32]{0:T(128)S(1)}, f32[32,18432]{1,0:T(8,128)}) fusion(f32[32]{0:T(128)S(1)} %broadcast_multiply_fusion, bf16[32,18432]{1,0:T(8,128)(2,1)} %param.9), kind=kLoop, calls=%fused_computation.2 | loop fusion | flops 2359264 | bytes 3539200 | tf_op jit(solution)/shard_map/reduce_sum | solution.py:31
  12.1 0.8 dynamic-slice
  12.9 1.7 fusion.4
  14.6 0.0 all-gather.2.cloned.1.call-update
  14.6 0.0 reduce-scatter.7.cloned.1.call-start
  14.7 52.0 %all-gather.2.cloned.1.call-done = bf16[512,2304]{1,0:T(8,128)(2,1)} async-done(((bf16[32,2304]{1,0:T(8,128)(2,1)}), bf16[512,2304]{1,0:T(8,128)(2,1)}) %all-gather.2.cloned.1.call-update) | async-done | bytes 2359312 | tf_op jit(solution)/shard_map/all_gather | solution.py:54
  66.7 2.4 fusion.12
  69.1 0.8 copy.28
  69.9 0.0 reduce-scatter.5.cloned.1.call-start
  69.9 4.8 %fusion.11 = f32[512,768]{1,0:T(8,128)} fusion(bf16[512,2304]{1,0:T(8,128)(2,1)} %all-gather.2.cloned.1.call-done, bf16[2304,768]{1,0:T(8,128)(2,1)S(1)} %copy-done), kind=kOutput, calls=%fused_computation.27 | convolution fusion | flops 1811939328 | bytes 7471104 | tf_op jit(solution)/shard_map/dot_general | solution.py:57
  74.8 2.7 reshape.64
  77.5 2.7 copy.38
  80.2 2.8 %reshape.65 = f32[512,768]{1,0:T(8,128)} reshape(f32[8,16,4,768]{3,2,1,0:T(4,128)} %bitcast.29) | data formatting | bytes 3145728 | tf_op jit(solution)/shard_map/reshape | solution.py:38
  83.0 0.0 reduce-scatter.5.cloned.1.call-update
  83.0 0.0 reduce-scatter.11.cloned.1.call-start
  83.1 10.6 %fusion.14 = f32[512,2304]{0,1:T(8,128)} fusion(bf16[512,2304]{1,0:T(8,128)(2,1)} %all-gather.2.cloned.1.call-done, bf16[2304,2304]{1,0:T(8,128)(2,1)} %param.14), kind=kOutput, calls=%fused_computation.30 | convolution fusion | flops 5435817984 | bytes 17694720 | tf_op jit(solution)/shard_map/dot_general | solution.py:60
  93.7 0.0 reduce-scatter.11.cloned.1.call-update
  93.7 0.0 reduce-scatter.9.cloned.1.call-start
  93.8 10.7 %fusion.13 = f32[512,2304]{0,1:T(8,128)} fusion(bf16[512,2304]{1,0:T(8,128)(2,1)} %all-gather.2.cloned.1.call-done, bf16[2304,2304]{1,0:T(8,128)(2,1)} %param.13), kind=kOutput, calls=%fused_computation.29 | convolution fusion | flops 5435817984 | bytes 17694720 | tf_op jit(solution)/shard_map/dot_general | solution.py:59
  104.4 0.0 reduce-scatter.9.cloned.1.call-update
  104.5 0.0 reduce-scatter.7.cloned.1.call-done
  104.5 1.4 convert_element_type.33
  105.9 8.5 %all-to-all-start.1 = ((bf16[16,4,32]{2,1,0:T(4,128)(2,1)}), bf16[16,4,32]{2,1,0:T(4,128)(2,1)S(1)}, u32[]{:S(2)}, u32[]{:S(2)}) async-start(bf16[16,4,32]{2,1,0:T(4,128)(2,1)} %bitcast.5), calls=%async_computation.3 | async-start | bytes 32768 | tf_op jit(solution)/shard_map/all_to_all | solution.py:89
  114.3 1.3 iota_compare_fusion
  115.6 6.0 %all-to-all-done.1 = bf16[16,4,32]{2,1,0:T(4,128)(2,1)S(1)} async-done(((bf16[16,4,32]{2,1,0:T(4,128)(2,1)}), bf16[16,4,32]{2,1,0:T(4,128)(2,1)S(1)}, u32[]{:S(2)}, u32[]{:S(2)}) %all-to-all-start.1) | async-done | bytes 4128 | tf_op jit(solution)/shard_map/all_to_all | solution.py:89
  121.6 0.6 copy-done.1
  122.2 0.7 copy.29
  122.9 0.7 all_to_all.46
  123.6 19.6 %reduce-scatter.5.cloned.1.call-done = f32[64,768]{1,0:T(8,128)} async-done(((f32[512,768]{1,0:T(8,128)}), f32[64,768]{1,0:T(8,128)}) %reduce-scatter.5.cloned.1.call-update) | async-done | bytes 196624 | tf_op jit(solution)/shard_map/reduce_scatter | solution.py:69
  143.2 1.6 convert_element_type.32
  144.8 1.6 all_to_all.40
  146.3 12.1 %all-to-all-start = ((bf16[16,4,768]{2,1,0:T(4,128)(2,1)}), bf16[16,4,768]{2,1,0:T(4,128)(2,1)}, u32[]{:S(2)}, u32[]{:S(2)}) async-start(bf16[16,4,768]{2,1,0:T(4,128)(2,1)} %all_to_all.40), calls=%async_computation.1 | async-start | bytes 196608 | tf_op jit(solution)/shard_map/all_to_all | solution.py:86
  158.4 0.7 slice_convert_fusion
  159.1 7.5 %all-to-all-done = bf16[16,4,768]{2,1,0:T(4,128)(2,1)} async-done(((bf16[16,4,768]{2,1,0:T(4,128)(2,1)}), bf16[16,4,768]{2,1,0:T(4,128)(2,1)}, u32[]{:S(2)}, u32[]{:S(2)}) %all-to-all-start) | async-done | bytes 98336 | tf_op jit(solution)/shard_map/all_to_all | solution.py:86
  166.6 1.5 copy.26
  168.1 1.6 reshape.66
  169.7 1.0 fusion.6
  170.7 1.8 fusion.10
  172.5 2.2 fusion.2
  174.8 1.7 all_to_all.47
  176.5 1.0 copy.30
  177.5 15.8 %all_to_all.54 = bf16[4,128,96]{2,0,1:T(4,128)(2,1)} all-to-all(bf16[4,128,96]{2,0,1:T(4,128)(2,1)S(1)} %copy.30), channel_id=1, replica_groups=mesh['wide'=16,'narrow'=8] {'wide','narrow'}, dimensions={1} | all-to-all | bytes 196608 | tf_op jit(solution)/shard_map/all_to_all | solution.py:94
  193.2 1.6 copy.31
  194.9 14.7 %reduce-scatter.11.cloned.1.call-done = f32[512,288]{0,1:T(8,128)} async-done(((f32[512,2304]{0,1:T(8,128)}), f32[512,288]{0,1:T(8,128)}) %reduce-scatter.11.cloned.1.call-update) | async-done | bytes 589840 | tf_op jit(solution)/shard_map/reduce_scatter | solution.py:82
  209.6 59.3 %reduce-scatter.9.cloned.1.call-done = f32[512,288]{0,1:T(8,128)} async-done(((f32[512,2304]{0,1:T(8,128)}), f32[512,288]{0,1:T(8,128)}) %reduce-scatter.9.cloned.1.call-update) | async-done | bytes 589840 | tf_op jit(solution)/shard_map/reduce_scatter | solution.py:81
  268.9 2.1 multiply_convert_fusion
  (7 shorter events, 0.1 us)
Async XLA Ops:
  7.2 62.8 %copy-start = (bf16[2304,768]{1,0:T(8,128)(2,1)S(1)}, bf16[2304,768]{1,0:T(8,128)(2,1)}, u32[]{:S(2)}) copy-start(bf16[2304,768]{1,0:T(8,128)(2,1)} %param.11) | copy-start | bytes 10616836
  7.2 59.5 %all-gather.2.cloned.1.call-start = ((), (), s32[]{:S(2)}) async-start(), calls=%async_computation.7 | async-start | bytes 2506752 | tf_op jit(solution)/shard_map/all_gather | solution.py:54
  14.6 89.8 %reduce-scatter.7.cloned.1.call-start = ((), (), s32[]{:S(2)}) async-start(), calls=%async_computation.9 | async-start | bytes 294912 | tf_op jit(solution)/shard_map/reduce_scatter | solution.py:75
  69.9 73.3 %reduce-scatter.5.cloned.1.call-start = ((), (), s32[]{:S(2)}) async-start(), calls=%async_computation.8 | async-start | bytes 1769472 | tf_op jit(solution)/shard_map/reduce_scatter | solution.py:69
  83.0 126.6 %reduce-scatter.11.cloned.1.call-start = ((), (), s32[]{:S(2)}) async-start(), calls=%async_computation.11 | async-start | bytes 5308416 | tf_op jit(solution)/shard_map/reduce_scatter | solution.py:82
  93.7 175.1 %reduce-scatter.9.cloned.1.call-start = ((), (), s32[]{:S(2)}) async-start(), calls=%async_computation.10 | async-start | bytes 5308416 | tf_op jit(solution)/shard_map/reduce_scatter | solution.py:81
  105.9 15.7 %all-to-all-start.1 = ((bf16[16,4,32]{2,1,0:T(4,128)(2,1)}), bf16[16,4,32]{2,1,0:T(4,128)(2,1)S(1)}, u32[]{:S(2)}, u32[]{:S(2)}) async-start(bf16[16,4,32]{2,1,0:T(4,128)(2,1)} %bitcast.5), calls=%async_computation.3 | async-start | bytes 32768 | tf_op jit(solution)/shard_map/all_to_all | solution.py:89
  121.6 0.6 copy-start.1
  146.3 20.2 %all-to-all-start = ((bf16[16,4,768]{2,1,0:T(4,128)(2,1)}), bf16[16,4,768]{2,1,0:T(4,128)(2,1)}, u32[]{:S(2)}, u32[]{:S(2)}) async-start(bf16[16,4,768]{2,1,0:T(4,128)(2,1)} %all_to_all.40), calls=%async_computation.1 | async-start | bytes 196608 | tf_op jit(solution)/shard_map/all_to_all | solution.py:86
Sparse Core Ops, SparseCore 0:
  14.8 51.8 all-gather.1
  70.0 30.7 reduce-scatter.6
  103.4 39.7 reduce-scatter.4
  145.6 63.9 reduce-scatter.10
  212.0 56.8 reduce-scatter.8
where the time goes:
time: 278 us
  waiting for transfers between devices  159 us (57%)
  matrix products  33.6 us (12%)
  local copies, waits for them, and re-layouts  20.9 us (8%)
  starting transfers between devices  20.7 us (7%)
  blocking collectives  15.8 us (6%)
  between operations  13.8 us (5%)
  other arithmetic  13.7 us (5%)
    reduce_scatter x1, waiting for transfers between devices, body(): lax.psum_scatter(gate_part, 'narrow', scatter_dimension=1, tiled=True)  59.3 us
    all_gather x1, waiting for transfers between devices, body(): piece = lax.all_gather(normed_part, 'wide', axis=0, tiled=True)  52 us
    reduce_scatter x1, waiting for transfers between devices, body(): lax.psum_scatter(narrow_major(query_part, n_wide, n_narrow, rows_dev), 'n...  19.6 us
    all_to_all x1, blocking collectives, body(): lax.all_to_all(attended, ('wide', 'narrow'), split_axis=1, concat_axis=0,...  15.8 us
    reduce_scatter x1, waiting for transfers between devices, body(): lax.psum_scatter(upper_part, 'narrow', scatter_dimension=1, tiled=True)  14.7 us
    all_to_all x1, starting transfers between devices, body(): lax.all_to_all(query_sum.astype(jnp.bfloat16), 'wide', split_axis=0, conc...  12.1 us
    dot_general x1, matrix products, body(): jnp.dot(piece, w_gate, preferred_element_type=jnp.float32)  10.7 us
    dot_general x1, matrix products, body(): jnp.dot(piece, w_up, preferred_element_type=jnp.float32)  10.6 us
  transfers between devices with their start and end apart: 7, of which 6 were waited for; matrix products, arithmetic and copies ran while one was open for 18% of the time, Pallas kernels for 0%

commit v1 on v0

v1 whole, which is shorter than its diff:
```python
import functools

import jax
import jax.numpy as jnp
from jax import lax
from jax.experimental import pallas as pl
from jax.experimental.pallas import tpu as pltpu
from jax.sharding import PartitionSpec as P

MESH = pl.DeviceIdType.MESH
F32 = jnp.float32
BF16 = jnp.bfloat16
UNITS = 8
LANES = 128
Q_SPLIT = (16, 16, 16, 8)
H_SPLIT = (80, 80, 64, 64)
MESSAGES = 10


def sum_scratch(split, dtype):
    a, b, xa, xb = split
    ab, xr = a + b, xa + xb
    n = UNITS
    return [
        pltpu.VMEM((n, 2, 4 * ab, LANES), dtype),
        pltpu.VMEM((n, 2, ab, LANES), dtype),
        pltpu.VMEM((n, 2, ab, LANES), dtype),
        pltpu.VMEM((n, 2, a, LANES), dtype),
        pltpu.VMEM((n, 2, b, LANES), dtype),
        pltpu.VMEM((n, 2, ab, LANES), dtype),
        pltpu.VMEM((n, ab, LANES), dtype),
        pltpu.VMEM((n, 2, 4, xr, LANES), dtype),
        pltpu.VMEM((n, 4, xr, LANES), dtype),
        pltpu.VMEM((n, 4 * xr, LANES), dtype),
        pltpu.VMEM((n, xr, LANES), dtype),
        pltpu.VMEM((n, xr, LANES), dtype),
        pltpu.VMEM((n, xa, LANES), dtype),
        pltpu.VMEM((n, xb, LANES), dtype),
        pltpu.SemaphoreType.DMA((n, MESSAGES)),
        pltpu.SemaphoreType.DMA((n, MESSAGES)),
    ]


class Summer:
    def __init__(self, split, dtype, refs, here, up, down, across):
        self.split, self.dtype = split, dtype
        (
            self.zbuf, self.z_up1, self.z_dn1, self.z_up2, self.z_dn2, self.fin, self.x_last,
            self.cbuf, self.c_in, self.xz, self.x_up1, self.x_dn1, self.x_up2, self.x_dn2,
            self.send, self.recv,
        ) = refs
        self.x, self.z = here
        self.up, self.down, self.across = up, down, across
        self.align = 16 if dtype == BF16 else 8

    def copy(self, k, t):
        a, b, xa, xb = self.split
        ab, xr = a + b, xa + xb
        src, dst, to = [
            (self.zbuf.at[t, :, 0:ab], self.z_up1.at[t], self.up),
            (self.zbuf.at[t, :, ab : 2 * ab], self.z_dn1.at[t], self.down),
            (self.cbuf.at[t, 1], self.c_in.at[t], self.across),
            (self.zbuf.at[t, :, 2 * ab : 2 * ab + a], self.z_up2.at[t], self.up),
            (self.zbuf.at[t, :, 2 * ab + a : 3 * ab], self.z_dn2.at[t], self.down),
            (self.xz.at[t, 0:xr], self.x_up1.at[t], self.up),
            (self.xz.at[t, xr : 2 * xr], self.x_dn1.at[t], self.down),
            (self.fin.at[t, 1], self.x_last.at[t], self.across),
            (self.xz.at[t, 2 * xr : 2 * xr + xa], self.x_up2.at[t], self.up),
            (self.xz.at[t, 2 * xr + xa : 3 * xr], self.x_dn2.at[t], self.down),
        ][k]
        return pltpu.make_async_remote_copy(
            src_ref=src, dst_ref=dst, send_sem=self.send.at[t, k], recv_sem=self.recv.at[t, k],
            device_id=to, device_id_type=MESH,
        )

    def places(self, a, b, z_to):
        dz = lax.rem(z_to - self.z + 4, 4)
        ab = a + b
        first = jnp.where(dz == 0, 3 * ab, jnp.where(dz == 1, 2 * ab, jnp.where(dz == 2, 0, a + 2 * b)))
        second = jnp.where(
            dz == 0, 3 * ab + a, jnp.where(dz == 1, a, jnp.where(dz == 2, ab, 2 * ab + a))
        )
        return first, second

    def at(self, start, size):
        return pl.ds(pl.multiple_of(start, self.align), size)

    def start_first(self, t):
        for k in (0, 1, 2):
            self.copy(k, t).start()

    def second(self, t):
        a, b, xa, xb = self.split
        ab, xr = a + b, xa + xb
        self.copy(0, t).wait_recv()
        for i in (0, 1):
            self.zbuf[t, i, 2 * ab : 2 * ab + a] = (
                self.zbuf[t, i, 2 * ab : 2 * ab + a].astype(F32) + self.z_up1[t, i, 0:a].astype(F32)
            ).astype(self.dtype)
        self.copy(3, t).start()
        self.copy(1, t).wait_recv()
        for i in (0, 1):
            self.zbuf[t, i, 2 * ab + a : 3 * ab] = (
                self.zbuf[t, i, 2 * ab + a : 3 * ab].astype(F32) + self.z_dn1[t, i, 0:b].astype(F32)
            ).astype(self.dtype)
        self.copy(4, t).start()
        self.copy(2, t).wait_recv()
        for z_to in range(4):
            first, second = self.places(xa, xb, z_to)
            both = (
                self.cbuf[t, 0, z_to].astype(F32) + self.c_in[t, z_to].astype(F32)
            ).astype(self.dtype)
            self.xz[t, self.at(first, xa)] = both[0:xa]
            self.xz[t, self.at(second, xb)] = both[xa:xr]
        self.copy(5, t).start()
        self.copy(6, t).start()

    def third(self, t):
        a, b, xa, xb = self.split
        ab, xr = a + b, xa + xb
        self.copy(3, t).wait_recv()
        self.copy(4, t).wait_recv()
        for i in (0, 1):
            place = jnp.where(self.x == i, 0, 1)
            self.fin[t, place, 0:a] = (
                self.zbuf[t, i, 3 * ab : 3 * ab + a].astype(F32)
                + self.z_up2[t, i].astype(F32)
                + self.z_dn1[t, i, b:ab].astype(F32)
            ).astype(self.dtype)
            self.fin[t, place, a:ab] = (
                self.zbuf[t, i, 3 * ab + a : 4 * ab].astype(F32)
                + self.z_dn2[t, i].astype(F32)
                + self.z_up1[t, i, a:ab].astype(F32)
            ).astype(self.dtype)
        self.copy(7, t).start()
        self.copy(5, t).wait_recv()
        self.xz[t, 2 * xr : 2 * xr + xa] = (
            self.xz[t, 2 * xr : 2 * xr + xa].astype(F32) + self.x_up1[t, 0:xa].astype(F32)
        ).astype(self.dtype)
        self.copy(8, t).start()
        self.copy(6, t).wait_recv()
        self.xz[t, 2 * xr + xa : 3 * xr] = (
            self.xz[t, 2 * xr + xa : 3 * xr].astype(F32) + self.x_dn1[t, 0:xb].astype(F32)
        ).astype(self.dtype)
        self.copy(9, t).start()

    def last(self, t):
        a, b, xa, xb = self.split
        ab, xr = a + b, xa + xb
        self.copy(7, t).wait_recv()
        one = self.fin[t, 0].astype(F32) + self.x_last[t].astype(F32)
        self.copy(8, t).wait_recv()
        self.copy(9, t).wait_recv()
        two = (
            self.xz[t, 3 * xr : 3 * xr + xa].astype(F32)
            + self.x_up2[t].astype(F32)
            + self.x_dn1[t, xb:xr].astype(F32)
        )
        three = (
            self.xz[t, 3 * xr + xa : 4 * xr].astype(F32)
            + self.x_dn2[t].astype(F32)
            + self.x_up1[t, xa:xr].astype(F32)
        )
        return one, two, three

    def finish(self, t):
        for k in range(MESSAGES):
            self.copy(k, t).wait_send()


def kernel(
    x_hbm, gain_hbm, wq_hbm, wkv_hbm, wg_hbm, wu_hbm, k_hbm, v_hbm, len_ref,
    att_ref, hid_ref,
    xbuf, gain, wq, wkv, wg, wu, keys, values, load_sem,
    piece, pbuf, ag_send, ag_recv, ag_side,
    qtmp, gtmp, utmp,
    qout, qin, q_send, q_recv,
    att1, att1_in, att1_send, att1_recv,
    att2, att2_in, att2_send, att2_recv,
    *sum_refs,
):
    w = lax.axis_index("wide")
    n = lax.axis_index("narrow")
    y, h, c = w // 4, lax.rem(w // 2, 2), lax.rem(w, 2)
    x, z = n // 4, lax.rem(n, 4)
    slab = piece.shape[3]
    tiles = slab // LANES
    rows = xbuf.shape[0]
    width = xbuf.shape[1]

    def wide(yy, hh, cc):
        return (yy * 2 + hh) * 2 + cc

    y_up = (wide(lax.rem(y + 1, 4), h, c), n)
    y_down = (wide(lax.rem(y + 3, 4), h, c), n)
    side = (wide(y, h, 1 - c), n)
    pair = (wide(y, 1 - h, c), (1 - x) * 4 + z)
    z_up = (w, x * 4 + lax.rem(z + 1, 4))
    z_down = (w, x * 4 + lax.rem(z + 3, 4))
    across = (w, (1 - x) * 4 + z)

    loads = [
        pltpu.make_async_copy(src, dst, load_sem.at[i])
        for i, (src, dst) in enumerate(
            [
                (x_hbm, xbuf), (gain_hbm, gain), (wq_hbm, wq), (wkv_hbm, wkv),
                (wg_hbm, wg), (wu_hbm, wu), (k_hbm, keys), (v_hbm, values),
            ]
        )
    ]
    for load in loads:
        load.start()

    barrier = pltpu.get_barrier_semaphore()
    for s in range(1, 16):
        pl.semaphore_signal(barrier, inc=1, device_id=(lax.rem(w + s, 16), n), device_id_type=MESH)
    for s in range(1, 8):
        pl.semaphore_signal(barrier, inc=1, device_id=(w, lax.rem(n + s, 8)), device_id_type=MESH)
    pl.semaphore_signal(barrier, inc=1, device_id=pair, device_id_type=MESH)

    loads[0].wait()
    loads[1].wait()
    step_cols = 1024

    def add_block(i, total):
        block = xbuf[:, pl.ds(pl.multiple_of(i * step_cols, step_cols), step_cols)].astype(F32)
        for s in range(step_cols // 256):
            total = total + block[:, s * 256 : (s + 1) * 256]
        return total

    zero = jnp.zeros((rows, 256), F32)
    total = lax.fori_loop(0, width // step_cols, add_block, zero)
    average = jnp.sum(total, axis=1, keepdims=True) * (1.0 / width)

    def add_square(i, total):
        block = xbuf[:, pl.ds(pl.multiple_of(i * step_cols, step_cols), step_cols)].astype(F32)
        block = block - average
        block = block * block
        for s in range(step_cols // 256):
            total = total + block[:, s * 256 : (s + 1) * 256]
        return total

    total = lax.fori_loop(0, width // step_cols, add_square, zero)
    spread = jnp.sum(total, axis=1, keepdims=True) * (1.0 / width)
    factor = lax.rsqrt(spread + 1e-05)

    def normed(owner, i):
        start = pl.multiple_of(owner * slab + i * LANES, LANES)
        block = xbuf[:, pl.ds(start, LANES)].astype(F32)
        return ((block - average) * factor * gain[pl.ds(owner * tiles + i, 1), :]).astype(BF16)

    pair_n = (1 - x) * 4 + z
    for i in range(tiles):
        pbuf[:, i * LANES : (i + 1) * LANES] = normed(pair_n, i)
    for i in range(tiles):
        piece[0, c, :, i * LANES : (i + 1) * LANES] = normed(n, i)

    pl.semaphore_wait(barrier, 23)

    def gather_copy(k):
        src, slot, to = [
            (pbuf, 1, pair),
            (piece.at[0, c], 2, y_up),
            (piece.at[0, c], 3, y_down),
            (piece.at[1, c], 4, y_up),
            (piece.at[1, c], 5, y_down),
            (piece.at[2, c], 6, y_up),
            (piece.at[5, c], 7, y_down),
        ][k]
        return pltpu.make_async_remote_copy(
            src_ref=src, dst_ref=piece.at[slot, c], send_sem=ag_send.at[k], recv_sem=ag_recv.at[k],
            device_id=to, device_id_type=MESH,
        )

    def side_copy(t):
        return pltpu.make_async_remote_copy(
            src_ref=piece.at[t, c], dst_ref=piece.at[t, c], send_sem=ag_send.at[7 + t],
            recv_sem=ag_side.at[t], device_id=side, device_id_type=MESH,
        )

    def side_wait(t):
        pltpu.make_async_remote_copy(
            src_ref=piece.at[t, 1 - c], dst_ref=piece.at[t, 1 - c], send_sem=ag_send.at[7 + t],
            recv_sem=ag_side.at[t], device_id=side, device_id_type=MESH,
        ).wait_recv()

    for k in (0, 1, 2):
        gather_copy(k).start()
    side_copy(0).start()

    count = len(sum_refs) // 2
    q_sum = Summer(Q_SPLIT, F32, sum_refs[:count], (x, z), z_up, z_down, across)
    h_sum = Summer(H_SPLIT, BF16, sum_refs[count:], (x, z), z_up, z_down, across)

    def chip_of(t):
        group, odd = t // 2, lax.rem(t, 2)
        dy = jnp.where(group == 0, 0, jnp.where(group == 3, 2, jnp.where(odd == 0, 3, 1)))
        flip = jnp.where((group == 0) | (group == 3), odd, group - 1)
        return lax.rem(y + dy, 4), lax.rem(h + flip, 2)

    def project_q(t):
        side_wait(t)
        piece_t = piece[t].reshape(2 * rows, slab)
        for s in range(3):
            qtmp[:, s * 256 : (s + 1) * 256] = jnp.dot(
                piece_t, wq[:, s * 256 : (s + 1) * 256], preferred_element_type=F32
            )
        qtmp[:, 768:896] = jnp.zeros((2 * rows, LANES), F32)
        qtmp[:, 768:800] = jnp.dot(piece_t, wkv[...], preferred_element_type=F32)
        qtmp[:, 768:896] = pltpu.roll(qtmp[:, 768:896], 32 * lax.rem(w, 4), axis=1)
        low = lax.broadcasted_iota(jnp.int32, (8, 896), 0) < 4
        for m in range(4):
            top = qtmp[8 * m : 8 * m + 8, :]
            bottom = qtmp[rows + 8 * m : rows + 8 * m + 8, :]
            even = jnp.where(low, top, pltpu.roll(bottom, 4, axis=0))
            odd = jnp.where(low, pltpu.roll(top, 4, axis=0), bottom)
            for to, block in ((2 * m, even), (2 * m + 1, odd)):
                x_to, z_to = to // 4, to % 4
                first, second = q_sum.places(16, 16, z_to)
                far = jnp.where(x == x_to, 0, 1)
                for s in range(2):
                    q_sum.zbuf[t, x_to, q_sum.at(first + 8 * s, 8)] = block[:, s * 128 : (s + 1) * 128]
                    q_sum.zbuf[t, x_to, q_sum.at(second + 8 * s, 8)] = block[
                        :, (2 + s) * 128 : (3 + s) * 128
                    ]
                for s in range(3):
                    q_sum.cbuf[t, far, z_to, 8 * s : 8 * s + 8] = block[:, (4 + s) * 128 : (5 + s) * 128]
        q_sum.start_first(t)

    def project_h(t):
        piece_t = piece[t].reshape(2 * rows, slab)
        for s in range(gtmp.shape[1] // 256):
            cols = slice(s * 256, (s + 1) * 256)
            gtmp[:, cols] = jnp.dot(piece_t, wg[:, cols], preferred_element_type=F32).astype(BF16)
            utmp[:, cols] = jnp.dot(piece_t, wu[:, cols], preferred_element_type=F32).astype(BF16)
        for to in range(8):
            x_to, z_to = to // 4, to % 4
            first, second = h_sum.places(80, 80, z_to)
            far = jnp.where(x == x_to, 0, 1)
            start = 288 * to
            base = start // LANES * LANES
            stop = min(-(-(start + 288) // LANES) * LANES, gtmp.shape[1])
            off = start - base
            g = gtmp[:, base:stop]
            u = utmp[:, base:stop]
            g0, g1, gr = g[:, off : off + 128], g[:, off + 128 : off + 256], g[:, off + 256 : off + 288]
            u0, u1, ur = u[:, off : off + 128], u[:, off + 128 : off + 256], u[:, off + 256 : off + 288]
            h_sum.zbuf[t, x_to, h_sum.at(first, 64)] = g0
            h_sum.zbuf[t, x_to, h_sum.at(first + 64, 16)] = g1[0:16]
            h_sum.zbuf[t, x_to, h_sum.at(second, 48)] = g1[16:64]
            h_sum.zbuf[t, x_to, h_sum.at(second + 48, 32)] = u0[0:32]
            h_sum.cbuf[t, far, z_to, 0:32] = u0[32:64]
            h_sum.cbuf[t, far, z_to, 32:96] = u1
            h_sum.cbuf[t, far, z_to, 96:128, 0:32] = gr[0:32]
            h_sum.cbuf[t, far, z_to, 96:128, 32:64] = ur[0:32]
            h_sum.cbuf[t, far, z_to, 96:128, 64:96] = gr[32:64]
            h_sum.cbuf[t, far, z_to, 96:128, 96:128] = ur[32:64]
        h_sum.start_first(t)

    def q_copy(t, core):
        yy, hh = chip_of(t)
        to = wide(yy, hh, core)
        return to, pltpu.make_async_remote_copy(
            src_ref=qout.at[t, core], dst_ref=qin.at[w], send_sem=q_send.at[t, core],
            recv_sem=q_recv.at[w], device_id=(to, n), device_id_type=MESH,
        )

    def finish_q(t):
        one, two, three = q_sum.last(t)
        blocks = [one[8 * s : 8 * s + 8] for s in range(4)]
        blocks += [two[0:8], two[8:16], three]
        blocks = [block.astype(BF16).astype(F32) for block in blocks]
        for core in range(2):
            for s, block in enumerate(blocks):
                qout[t, core, :, s * 128 : (s + 1) * 128] = block[4 * core : 4 * core + 4]
            to, copy = q_copy(t, core)

            @pl.when(to != w)
            def _():
                copy.start()

            @pl.when(to == w)
            def _():
                for s, block in enumerate(blocks):
                    qin[w, :, s * 128 : (s + 1) * 128] = block[4 * core : 4 * core + 4]

    def silu(v):
        return v / (1.0 + jnp.exp(-v))

    def finish_h(t):
        one, two, three = h_sum.last(t)
        yy, hh = chip_of(t)
        start = (yy * 2 + hh) * 64

        def out_rows(offset, size):
            return pl.ds(pl.multiple_of(start + offset, 32), size)

        hid_ref[out_rows(0, 32), 0:128] = (silu(one[0:32]) * one[128:160]).astype(BF16)
        hid_ref[out_rows(32, 32), 0:128] = (silu(one[32:64]) * two[0:32]).astype(BF16)
        hid_ref[out_rows(0, 32), 128:256] = (silu(one[64:96]) * two[32:64]).astype(BF16)
        hid_ref[out_rows(32, 32), 128:256] = (silu(one[96:128]) * three[0:32]).astype(BF16)
        rest = three[32:64]
        rest = silu(rest) * pltpu.roll(rest, 96, axis=1)
        hid_ref[out_rows(0, 32), 256:288] = rest[:, 0:32].astype(BF16)
        hid_ref[out_rows(32, 32), 256:288] = pltpu.roll(rest, 64, axis=1)[:, 0:32].astype(BF16)

    def att1_copy(s):
        to = lax.rem(n + s, 8)
        return pltpu.make_async_remote_copy(
            src_ref=att1.at[to], dst_ref=att1_in.at[n], send_sem=att1_send.at[s],
            recv_sem=att1_recv.at[s], device_id=(w, to), device_id_type=MESH,
        )

    def att2_copy(s):
        to = lax.rem(w + s, 16)
        return pltpu.make_async_remote_copy(
            src_ref=att2.at[to], dst_ref=att2_in.at[w], send_sem=att2_send.at[s],
            recv_sem=att2_recv.at[s], device_id=(to, n), device_id_type=MESH,
        )

    def attend():
        loads[6].wait()
        loads[7].wait()

        @pl.loop(1, 16)
        def _(s):
            source = lax.rem(w + s, 16)
            pltpu.make_async_remote_copy(
                src_ref=qin.at[source], dst_ref=qin.at[source], send_sem=q_send.at[0, 0],
                recv_sem=q_recv.at[source], device_id=side, device_id_type=MESH,
            ).wait_recv()

        scale = 256 ** (-0.5)
        for r in range(4):
            heads = jnp.concatenate(
                [qin[:, r, s * 256 : (s + 1) * 256] for s in range(3)], axis=0
            )
            kv = qin[:, r, 768:896]
            kv = [jnp.sum(kv[4 * i : 4 * i + 4], axis=0, keepdims=True) for i in range(4)]
            own_key = jnp.concatenate(kv[0:2], axis=1)
            own_value = jnp.concatenate(kv[2:4], axis=1)
            scores = lax.dot_general(
                heads.astype(BF16), keys[r], (((1,), (1,)), ((), ())), preferred_element_type=F32
            ) * scale
            valid = lax.broadcasted_iota(jnp.int32, scores.shape, 1) < len_ref[r]
            raised = jnp.where(valid, jnp.exp(scores), 0.0)
            own = jnp.exp(jnp.sum(heads * own_key, axis=1, keepdims=True) * scale)
            total = jnp.sum(raised, axis=1, keepdims=True) + own
            probs = (raised / total).astype(BF16)
            own_prob = (own / total).astype(BF16).astype(F32)
            out = jnp.dot(probs, values[r], preferred_element_type=F32) + own_prob * own_value
            flat = jnp.concatenate(
                [out[0:16], out[16:32], out[32:48], jnp.zeros((16, LANES), F32)], axis=1
            )
            for to in range(8):
                att1[to, r] = flat[:, 96 * to : 96 * to + 128].astype(BF16)
        att1_in[n] = att1[n]
        for s in range(1, 8):
            att1_copy(s).start()

    def spread_heads():
        for s in range(1, 8):
            source = lax.rem(n + 8 - s, 8)
            pltpu.make_async_remote_copy(
                src_ref=att1.at[source], dst_ref=att1_in.at[source], send_sem=att1_send.at[s],
                recv_sem=att1_recv.at[s], device_id=(w, source), device_id_type=MESH,
            ).wait_recv()
        att2[...] = jnp.swapaxes(att1_in[...].reshape(32, 16, LANES), 0, 1)
        att2_in[w] = att2[w]
        for s in range(1, 16):
            att2_copy(s).start()

    def gather_heads():
        for s in range(1, 16):
            source = lax.rem(w + 16 - s, 16)
            pltpu.make_async_remote_copy(
                src_ref=att2.at[source], dst_ref=att2_in.at[source], send_sem=att2_send.at[s],
                recv_sem=att2_recv.at[s], device_id=(source, n), device_id_type=MESH,
            ).wait_recv()
        att_ref[...] = att2_in[...].reshape(512, LANES)[:, 0:96]

    def unit(j):
        is_q = (j < 6) | (j == 7) | (j == 8)
        t = jnp.where(j < 6, j, jnp.where(is_q, j - 1, jnp.where(j == 6, 0, j - 8)))
        return is_q, t

    def stage(j, q_step, h_step):
        real = (j >= 0) & (j < 16)
        is_q, t = unit(j)

        @pl.when(real & is_q)
        def _():
            q_step(t)

        @pl.when(real & jnp.logical_not(is_q))
        def _():
            h_step(t)

    loads[2].wait()
    loads[3].wait()

    @pl.loop(0, 19)
    def _(j):
        @pl.when(j == 6)
        def _():
            loads[4].wait()
            loads[5].wait()

        stage(j, project_q, project_h)

        @pl.when(j == 0)
        def _():
            gather_copy(0).wait_recv()
            side_copy(1).start()
            gather_copy(3).start()
            gather_copy(4).start()
            gather_copy(1).wait_recv()
            side_copy(2).start()
            gather_copy(5).start()
            gather_copy(2).wait_recv()
            side_copy(3).start()

        @pl.when(j == 3)
        def _():
            gather_copy(4).wait_recv()
            side_copy(5).start()
            gather_copy(6).start()
            gather_copy(3).wait_recv()
            side_copy(4).start()

        @pl.when(j == 6)
        def _():
            gather_copy(5).wait_recv()
            side_copy(6).start()
            gather_copy(6).wait_recv()
            side_copy(7).start()

        stage(j - 1, q_sum.second, h_sum.second)
        stage(j - 2, q_sum.third, h_sum.third)
        stage(j - 3, finish_q, finish_h)

        @pl.when(j == 13)
        def _():
            attend()

        @pl.when(j == 15)
        def _():
            spread_heads()

    gather_heads()

    for k in range(7):
        gather_copy(k).wait_send()
    for t in range(8):
        side_copy(t).wait_send()

    @pl.loop(0, 8)
    def _(t):
        q_sum.finish(t)
        h_sum.finish(t)
        for core in range(2):
            to, copy = q_copy(t, core)

            @pl.when(to != w)
            def _():
                copy.wait_send()

    for s in range(1, 8):
        att1_copy(s).wait_send()
    for s in range(1, 16):
        att2_copy(s).wait_send()


def body(
    layer_input, norm_gain, w_query, w_keyvalue, w_gate, w_up, key_cache, value_cache, cache_lengths
):
    rows, width = layer_input.shape
    slab = w_query.shape[0]
    anywhere = pl.BlockSpec(memory_space=pl.ANY)
    vmem = pl.BlockSpec(memory_space=pltpu.VMEM)
    dma = pltpu.SemaphoreType.DMA
    attended, hidden = pl.pallas_call(
        kernel,
        out_shape=(
            jax.ShapeDtypeStruct((512, 96), BF16),
            jax.ShapeDtypeStruct((512, 288), BF16),
        ),
        in_specs=[anywhere] * 8 + [pl.BlockSpec(memory_space=pltpu.SMEM)],
        out_specs=(vmem, vmem),
        scratch_shapes=[
            pltpu.VMEM((rows, width), BF16),
            pltpu.VMEM((width // LANES, LANES), F32),
            pltpu.VMEM(w_query.shape, BF16),
            pltpu.VMEM(w_keyvalue.shape, BF16),
            pltpu.VMEM(w_gate.shape, BF16),
            pltpu.VMEM(w_up.shape, BF16),
            pltpu.VMEM(key_cache.shape, BF16),
            pltpu.VMEM(value_cache.shape, BF16),
            dma((8,)),
            pltpu.VMEM((UNITS, 2, rows, slab), BF16),
            pltpu.VMEM((rows, slab), BF16),
            dma((15,)),
            dma((7,)),
            dma((8,)),
            pltpu.VMEM((2 * rows, 896), F32),
            pltpu.VMEM((2 * rows, w_gate.shape[1]), BF16),
            pltpu.VMEM((2 * rows, w_up.shape[1]), BF16),
            pltpu.VMEM((UNITS, 2, 4, 896), F32),
            pltpu.VMEM((16, 4, 896), F32),
            dma((UNITS, 2)),
            dma((16,)),
            pltpu.VMEM((8, 4, 16, LANES), BF16),
            pltpu.VMEM((8, 4, 16, LANES), BF16),
            dma((8,)),
            dma((8,)),
            pltpu.VMEM((16, 32, LANES), BF16),
            pltpu.VMEM((16, 32, LANES), BF16),
            dma((16,)),
            dma((16,)),
        ]
        + sum_scratch(Q_SPLIT, F32)
        + sum_scratch(H_SPLIT, BF16),
        compiler_params=pltpu.CompilerParams(
            collective_id=0, has_side_effects=True, vmem_limit_bytes=60 * 1024 * 1024
        ),
    )(
        layer_input, norm_gain.reshape(width // LANES, LANES), w_query, w_keyvalue, w_gate, w_up,
        key_cache, value_cache, cache_lengths,
    )
    return attended, hidden


def solution(mesh):
    placed = (
        P("wide", None),
        P(),
        P("narrow", "wide"),
        P("narrow", "wide"),
        P("narrow", "wide"),
        P("narrow", "wide"),
        P(("wide", "narrow"), None, None),
        P(("wide", "narrow"), None, None),
        P(("wide", "narrow")),
    )
    return jax.shard_map(
        body,
        mesh=mesh,
        in_specs=placed,
        out_specs=(P(None, ("wide", "narrow")), P(None, ("wide", "narrow"))),
        check_vma=False,
    )
```

time: 278 us -> 96.7 us (0.35)
  the two profiles are of different devices: /device:TPU:1 before, /device:TPU:2 now
where the time goes in v1:
time: 96.7 us; the launch traced here: 96.5 us
  Pallas kernels  90.4 us (93%)
  local copies, waits for them, and re-layouts  5.47 us (6%)
    pallas_call x1, Pallas kernels, body(): pl.pallas_call(kernel, out_shape=(jax.ShapeDtypeStruct((512, 96), BF16),...  90.4 us
    pallas_call x2, local copies, waits for them, and re-layouts, body(): pl.pallas_call(kernel, out_shape=(jax.ShapeDtypeStruct((512, 96), BF16),...  3.5 us
    unnamed x1, local copies, waits for them, and re-layouts  1.97 us

profile of v1, /device:TPU:2, one launch (start us, length us, event | category | flops | bytes accessed | tf_op | source)
XLA Modules:
  0.0 96.5 jit_solution(17258889686801937130)
XLA Ops:
  0.6 2.0 %copy.11.wkv_hbm = bf16[2304,32]{1,0:T(8,128)(2,1)} copy(bf16[2304,32]{0,1:T(8,128)(2,1)} %param.12) | data formatting | bytes 294912 | tf_op args[3]
  2.6 90.4 %shard_map.104 = (bf16[512,96]{1,0:T(8,128)(2,1)}, bf16[512,288]{1,0:T(8,128)(2,1)}) custom-call(bf16[32,18432]{1,0:T(8,128)(2,1)} %x_hbm.1, f32[144,128]{1,0:T(8,128)} %bitcast.1, bf16[2304,768]{1,0:T(8,128)(2,1)} %wq_hbm.1, bf16[2304,32]{1,0:T(8,128)(2,1)} %copy.11.wkv_hbm, bf16[2304,2304]{1,0:T(8,128)(2,1)} %wg_hbm.1, bf16[2304,2304]{1,0:T(8,128)(2,1)} %wu_hbm.1, ...), custom_call_target="tpu_custom_call" | custom-call | tf_op jit(solution)/shard_map/pallas_call | solution.py:582
  93.0 1.6 %copy.12 = bf16[512,96]{0,1:T(8,128)(2,1)} copy(bf16[512,96]{1,0:T(8,128)(2,1)} %get-tuple-element.2) | data formatting | bytes 196608 | tf_op jit(solution)/shard_map/pallas_call | solution.py:582
  94.6 1.9 %copy.13 = bf16[512,288]{0,1:T(8,128)(2,1)} copy(bf16[512,288]{1,0:T(8,128)(2,1)} %get-tuple-element.3) | data formatting | bytes 589824 | tf_op jit(solution)/shard_map/pallas_call | solution.py:582

commit v2 on v1

--- a/solution.py
+++ b/solution.py
@@ -15,6 +15,37 @@
 Q_SPLIT = (16, 16, 16, 8)
 H_SPLIT = (80, 80, 64, 64)
 MESSAGES = 10
+PARTS = 3
+GATHER = {
+    1: (1, 1), 2: (2, 2), 4: (5, 1), 5: (4, 1), 6: (6, 1), 8: (7, 1),
+}
+Q_PROJECT = {
+    0: (0, 1), 2: (1, 1), 3: (2, 2), 8: (4, 2), 9: (6, 2),
+}
+H_PROJECT = {
+    4: (0, 2), 9: (6, 2), 15: (4, 2), 18: (2, 2),
+}
+Q_SECOND = {
+    1: (0, 1), 6: (1, 1), 7: (3, 1), 8: (2, 1), 12: (5, 1), 13: (4, 1), 14: (6, 2),
+}
+Q_THIRD = {
+    3: (0, 1), 10: (3, 1), 11: (2, 1), 12: (1, 1), 16: (4, 1), 17: (5, 3),
+}
+H_SECOND = {
+    9: (0, 1), 16: (1, 1), 17: (6, 2), 23: (4, 2), 24: (3, 1), 25: (2, 1),
+}
+H_THIRD = {
+    23: (6, 1), 25: (7, 1), 26: (0, 1), 27: (4, 2), 28: (3, 1), 29: (1, 1), 30: (2, 1),
+}
+Q_LAST = {
+    15: (3, 1), 16: (1, 1), 18: (4, 1), 19: (0, 1), 20: (7, 1), 21: (5, 2), 22: (2, 1),
+}
+H_LAST = {
+    30: (6, 2), 31: (0, 1), 32: (4, 2), 33: (3, 1), 34: (1, 2),
+}
+ATTEND = 23
+SPREAD = 29
+PASSES = 35
 
 
 def sum_scratch(split, dtype):
@@ -36,7 +67,7 @@
         pltpu.VMEM((n, xr, LANES), dtype),
         pltpu.VMEM((n, xa, LANES), dtype),
         pltpu.VMEM((n, xb, LANES), dtype),
-        pltpu.SemaphoreType.DMA((n, MESSAGES)),
+        pltpu.SemaphoreType.DMA((MESSAGES,)),
         pltpu.SemaphoreType.DMA((n, MESSAGES)),
     ]
 
@@ -69,7 +100,7 @@
             (self.xz.at[t, 2 * xr + xa : 3 * xr], self.x_dn2.at[t], self.down),
         ][k]
         return pltpu.make_async_remote_copy(
-            src_ref=src, dst_ref=dst, send_sem=self.send.at[t, k], recv_sem=self.recv.at[t, k],
+            src_ref=src, dst_ref=dst, send_sem=self.send.at[k], recv_sem=self.recv.at[0 if isinstance(t, slice) else t, k],
             device_id=to, device_id_type=MESH,
         )
 
@@ -163,14 +194,14 @@
         )
         return one, two, three
 
-    def finish(self, t):
+    def finish(self):
         for k in range(MESSAGES):
-            self.copy(k, t).wait_send()
+            self.copy(k, slice(0, UNITS)).wait_send()
 
 
 def kernel(
     x_hbm, gain_hbm, wq_hbm, wkv_hbm, wg_hbm, wu_hbm, k_hbm, v_hbm, len_ref,
-    att_ref, hid_ref,
+    att_ref, hid,
     xbuf, gain, wq, wkv, wg, wu, keys, values, load_sem,
     piece, pbuf, ag_send, ag_recv, ag_side,
     qtmp, gtmp, utmp,
@@ -195,20 +226,19 @@
     y_down = (wide(lax.rem(y + 3, 4), h, c), n)
     side = (wide(y, h, 1 - c), n)
     pair = (wide(y, 1 - h, c), (1 - x) * 4 + z)
+    pair_up = (wide(lax.rem(y + 1, 4), 1 - h, c), (1 - x) * 4 + z)
+    pair_down = (wide(lax.rem(y + 3, 4), 1 - h, c), (1 - x) * 4 + z)
     z_up = (w, x * 4 + lax.rem(z + 1, 4))
     z_down = (w, x * 4 + lax.rem(z + 3, 4))
     across = (w, (1 - x) * 4 + z)
 
-    loads = [
-        pltpu.make_async_copy(src, dst, load_sem.at[i])
-        for i, (src, dst) in enumerate(
-            [
-                (x_hbm, xbuf), (gain_hbm, gain), (wq_hbm, wq), (wkv_hbm, wkv),
-                (wg_hbm, wg), (wu_hbm, wu), (k_hbm, keys), (v_hbm, values),
-            ]
-        )
-    ]
-    for load in loads:
+    part = wg.shape[1] // PARTS
+    pairs = [(x_hbm, xbuf), (gain_hbm, gain), (wq_hbm, wq), (wkv_hbm, wkv), (k_hbm, keys), (v_hbm, values)]
+    for i in range(PARTS):
+        cols = slice(i * part, (i + 1) * part)
+        pairs += [(wg_hbm.at[:, cols], wg.at[:, cols]), (wu_hbm.at[:, cols], wu.at[:, cols])]
+    loads = [pltpu.make_async_copy(src, dst, load_sem.at[i]) for i, (src, dst) in enumerate(pairs)]
+    for load in loads[0:4]:
         load.start()
 
     barrier = pltpu.get_barrier_semaphore()
@@ -216,10 +246,13 @@
         pl.semaphore_signal(barrier, inc=1, device_id=(lax.rem(w + s, 16), n), device_id_type=MESH)
     for s in range(1, 8):
         pl.semaphore_signal(barrier, inc=1, device_id=(w, lax.rem(n + s, 8)), device_id_type=MESH)
-    pl.semaphore_signal(barrier, inc=1, device_id=pair, device_id_type=MESH)
+    for other in (pair, pair_up, pair_down):
+        pl.semaphore_signal(barrier, inc=1, device_id=other, device_id_type=MESH)
 
     loads[0].wait()
     loads[1].wait()
+    for load in loads[6:]:
+        load.start()
     step_cols = 1024
 
     def add_block(i, total):
@@ -255,38 +288,38 @@
     for i in range(tiles):
         piece[0, c, :, i * LANES : (i + 1) * LANES] = normed(n, i)
 
-    pl.semaphore_wait(barrier, 23)
+    pl.semaphore_wait(barrier, 25)
 
     def gather_copy(k):
         src, slot, to = [
             (pbuf, 1, pair),
             (piece.at[0, c], 2, y_up),
             (piece.at[0, c], 3, y_down),
-            (piece.at[1, c], 4, y_up),
-            (piece.at[1, c], 5, y_down),
+            (pbuf, 4, pair_up),
+            (pbuf, 5, pair_down),
             (piece.at[2, c], 6, y_up),
             (piece.at[5, c], 7, y_down),
         ][k]
         return pltpu.make_async_remote_copy(
-            src_ref=src, dst_ref=piece.at[slot, c], send_sem=ag_send.at[k], recv_sem=ag_recv.at[k],
+            src_ref=src, dst_ref=piece.at[slot, c], send_sem=ag_send.at[0], recv_sem=ag_recv.at[k],
             device_id=to, device_id_type=MESH,
         )
 
     def side_copy(t):
         return pltpu.make_async_remote_copy(
-            src_ref=piece.at[t, c], dst_ref=piece.at[t, c], send_sem=ag_send.at[7 + t],
+            src_ref=piece.at[t, c], dst_ref=piece.at[t, c], send_sem=ag_send.at[1],
             recv_sem=ag_side.at[t], device_id=side, device_id_type=MESH,
         )
 
     def side_wait(t):
         pltpu.make_async_remote_copy(
-            src_ref=piece.at[t, 1 - c], dst_ref=piece.at[t, 1 - c], send_sem=ag_send.at[7 + t],
+            src_ref=piece.at[t, 1 - c], dst_ref=piece.at[t, 1 - c], send_sem=ag_send.at[1],
             recv_sem=ag_side.at[t], device_id=side, device_id_type=MESH,
         ).wait_recv()
 
-    for k in (0, 1, 2):
+    side_copy(0).start()
+    for k in (1, 2, 0, 3, 4):
         gather_copy(k).start()
-    side_copy(0).start()
 
     count = len(sum_refs) // 2
     q_sum = Summer(Q_SPLIT, F32, sum_refs[:count], (x, z), z_up, z_down, across)
@@ -298,20 +331,26 @@
         flip = jnp.where((group == 0) | (group == 3), odd, group - 1)
         return lax.rem(y + dy, 4), lax.rem(h + flip, 2)
 
-    def project_q(t):
-        side_wait(t)
-        piece_t = piece[t].reshape(2 * rows, slab)
+    def project_q(t, count):
+        size = count * 2 * rows
+        for u in range(count):
+            side_wait(t + u)
+        block = piece[pl.ds(t, count)].reshape(size, slab)
         for s in range(3):
-            qtmp[:, s * 256 : (s + 1) * 256] = jnp.dot(
-                piece_t, wq[:, s * 256 : (s + 1) * 256], preferred_element_type=F32
+            qtmp[0:size, s * 256 : (s + 1) * 256] = jnp.dot(
+                block, wq[:, s * 256 : (s + 1) * 256], preferred_element_type=F32
             )
-        qtmp[:, 768:896] = jnp.zeros((2 * rows, LANES), F32)
-        qtmp[:, 768:800] = jnp.dot(piece_t, wkv[...], preferred_element_type=F32)
-        qtmp[:, 768:896] = pltpu.roll(qtmp[:, 768:896], 32 * lax.rem(w, 4), axis=1)
+        qtmp[0:size, 768:896] = jnp.zeros((size, LANES), F32)
+        qtmp[0:size, 768:800] = lax.dot_general(
+            block, wkv[...], (((1,), (1,)), ((), ())), preferred_element_type=F32
+        )
+        qtmp[0:size, 768:896] = pltpu.roll(qtmp[0:size, 768:896], 32 * lax.rem(w, 4), axis=1)
+
+    def pack_q(t, base):
         low = lax.broadcasted_iota(jnp.int32, (8, 896), 0) < 4
         for m in range(4):
-            top = qtmp[8 * m : 8 * m + 8, :]
-            bottom = qtmp[rows + 8 * m : rows + 8 * m + 8, :]
+            top = qtmp[pl.ds(pl.multiple_of(base + 8 * m, 8), 8), :]
+            bottom = qtmp[pl.ds(pl.multiple_of(base + rows + 8 * m, 8), 8), :]
             even = jnp.where(low, top, pltpu.roll(bottom, 4, axis=0))
             odd = jnp.where(low, pltpu.roll(top, 4, axis=0), bottom)
             for to, block in ((2 * m, even), (2 * m + 1, odd)):
@@ -327,12 +366,35 @@
                     q_sum.cbuf[t, far, z_to, 8 * s : 8 * s + 8] = block[:, (4 + s) * 128 : (5 + s) * 128]
         q_sum.start_first(t)
 
-    def project_h(t):
-        piece_t = piece[t].reshape(2 * rows, slab)
+    def pass_on(t):
+        pltpu.make_async_remote_copy(
+            src_ref=pbuf, dst_ref=piece.at[t, c], send_sem=ag_send.at[0],
+            recv_sem=ag_recv.at[t - 1], device_id=side, device_id_type=MESH,
+        ).wait_recv()
+        side_copy(t).start()
+        for slot, k in ((2, 5), (5, 6)):
+
+            @pl.when(t == slot)
+            def _():
+                gather_copy(k).start()
+
+    def project_h(t, count, first):
+        size = count * 2 * rows
+        block = piece[pl.ds(t, count)].reshape(size, slab)
         for s in range(gtmp.shape[1] // 256):
+            if s * 256 % part == 0:
+
+                @pl.when(first)
+                def _():
+                    loads[6 + 2 * (s * 256 // part)].wait()
+                    loads[7 + 2 * (s * 256 // part)].wait()
+
+
             cols = slice(s * 256, (s + 1) * 256)
-            gtmp[:, cols] = jnp.dot(piece_t, wg[:, cols], preferred_element_type=F32).astype(BF16)
-            utmp[:, cols] = jnp.dot(piece_t, wu[:, cols], preferred_element_type=F32).astype(BF16)
+            gtmp[0:size, cols] = jnp.dot(block, wg[:, cols], preferred_element_type=F32).astype(BF16)
+            utmp[0:size, cols] = jnp.dot(block, wu[:, cols], preferred_element_type=F32).astype(BF16)
+
+    def pack_h(t, low):
         for to in range(8):
             x_to, z_to = to // 4, to % 4
             first, second = h_sum.places(80, 80, z_to)
@@ -341,8 +403,8 @@
             base = start // LANES * LANES
             stop = min(-(-(start + 288) // LANES) * LANES, gtmp.shape[1])
             off = start - base
-            g = gtmp[:, base:stop]
-            u = utmp[:, base:stop]
+            g = gtmp[pl.ds(pl.multiple_of(low, 64), 2 * rows), base:stop]
+            u = utmp[pl.ds(pl.multiple_of(low, 64), 2 * rows), base:stop]
             g0, g1, gr = g[:, off : off + 128], g[:, off + 128 : off + 256], g[:, off + 256 : off + 288]
             u0, u1, ur = u[:, off : off + 128], u[:, off + 128 : off + 256], u[:, off + 256 : off + 288]
             h_sum.zbuf[t, x_to, h_sum.at(first, 64)] = g0
@@ -361,8 +423,8 @@
         yy, hh = chip_of(t)
         to = wide(yy, hh, core)
         return to, pltpu.make_async_remote_copy(
-            src_ref=qout.at[t, core], dst_ref=qin.at[w], send_sem=q_send.at[t, core],
-            recv_sem=q_recv.at[w], device_id=(to, n), device_id_type=MESH,
+            src_ref=qout.at[t, core], dst_ref=qin.at[w], send_sem=q_send.at[0],
+            recv_sem=q_recv.at[0], device_id=(to, n), device_id_type=MESH,
         )
 
     def finish_q(t):
@@ -395,40 +457,41 @@
         def out_rows(offset, size):
             return pl.ds(pl.multiple_of(start + offset, 32), size)
 
-        hid_ref[out_rows(0, 32), 0:128] = (silu(one[0:32]) * one[128:160]).astype(BF16)
-        hid_ref[out_rows(32, 32), 0:128] = (silu(one[32:64]) * two[0:32]).astype(BF16)
-        hid_ref[out_rows(0, 32), 128:256] = (silu(one[64:96]) * two[32:64]).astype(BF16)
-        hid_ref[out_rows(32, 32), 128:256] = (silu(one[96:128]) * three[0:32]).astype(BF16)
+        hid[out_rows(0, 32), 0:128] = (silu(one[0:32]) * one[128:160]).astype(BF16)
+        hid[out_rows(32, 32), 0:128] = (silu(one[32:64]) * two[0:32]).astype(BF16)
+        hid[out_rows(0, 32), 128:256] = (silu(one[64:96]) * two[32:64]).astype(BF16)
+        hid[out_rows(32, 32), 128:256] = (silu(one[96:128]) * three[0:32]).astype(BF16)
         rest = three[32:64]
         rest = silu(rest) * pltpu.roll(rest, 96, axis=1)
-        hid_ref[out_rows(0, 32), 256:288] = rest[:, 0:32].astype(BF16)
-        hid_ref[out_rows(32, 32), 256:288] = pltpu.roll(rest, 64, axis=1)[:, 0:32].astype(BF16)
+        hid[out_rows(0, 32), 256:288] = rest[:, 0:32].astype(BF16)
+        hid[out_rows(32, 32), 256:288] = pltpu.roll(rest, 64, axis=1)[:, 0:32].astype(BF16)
+
+    def wait_all(buffer, send, recv):
+        part = buffer.at[0 : buffer.shape[0] - 1]
+        return pltpu.make_async_remote_copy(
+            src_ref=part, dst_ref=part, send_sem=send.at[0], recv_sem=recv.at[0],
+            device_id=side, device_id_type=MESH,
+        )
 
     def att1_copy(s):
         to = lax.rem(n + s, 8)
         return pltpu.make_async_remote_copy(
-            src_ref=att1.at[to], dst_ref=att1_in.at[n], send_sem=att1_send.at[s],
-            recv_sem=att1_recv.at[s], device_id=(w, to), device_id_type=MESH,
+            src_ref=att1.at[to], dst_ref=att1_in.at[n], send_sem=att1_send.at[0],
+            recv_sem=att1_recv.at[0], device_id=(w, to), device_id_type=MESH,
         )
 
     def att2_copy(s):
         to = lax.rem(w + s, 16)
         return pltpu.make_async_remote_copy(
-            src_ref=att2.at[to], dst_ref=att2_in.at[w], send_sem=att2_send.at[s],
-            recv_sem=att2_recv.at[s], device_id=(to, n), device_id_type=MESH,
+            src_ref=att2.at[to], dst_ref=att2_in.at[w], send_sem=att2_send.at[0],
+            recv_sem=att2_recv.at[0], device_id=(to, n), device_id_type=MESH,
         )
 
     def attend():
-        loads[6].wait()
-        loads[7].wait()
-
-        @pl.loop(1, 16)
-        def _(s):
-            source = lax.rem(w + s, 16)
-            pltpu.make_async_remote_copy(
-                src_ref=qin.at[source], dst_ref=qin.at[source], send_sem=q_send.at[0, 0],
-                recv_sem=q_recv.at[source], device_id=side, device_id_type=MESH,
-            ).wait_recv()
+        loads[4].wait()
+        loads[5].wait()
+
+        wait_all(qin, q_send, q_recv).wait_recv()
 
         scale = 256 ** (-0.5)
         for r in range(4):
@@ -459,116 +522,93 @@
             att1_copy(s).start()
 
     def spread_heads():
-        for s in range(1, 8):
-            source = lax.rem(n + 8 - s, 8)
-            pltpu.make_async_remote_copy(
-                src_ref=att1.at[source], dst_ref=att1_in.at[source], send_sem=att1_send.at[s],
-                recv_sem=att1_recv.at[s], device_id=(w, source), device_id_type=MESH,
-            ).wait_recv()
+        wait_all(att1_in, att1_send, att1_recv).wait_recv()
         att2[...] = jnp.swapaxes(att1_in[...].reshape(32, 16, LANES), 0, 1)
         att2_in[w] = att2[w]
         for s in range(1, 16):
             att2_copy(s).start()
 
     def gather_heads():
-        for s in range(1, 16):
-            source = lax.rem(w + 16 - s, 16)
-            pltpu.make_async_remote_copy(
-                src_ref=att2.at[source], dst_ref=att2_in.at[source], send_sem=att2_send.at[s],
-                recv_sem=att2_recv.at[s], device_id=(source, n), device_id_type=MESH,
-            ).wait_recv()
-        att_ref[...] = att2_in[...].reshape(512, LANES)[:, 0:96]
-
-    def unit(j):
-        is_q = (j < 6) | (j == 7) | (j == 8)
-        t = jnp.where(j < 6, j, jnp.where(is_q, j - 1, jnp.where(j == 6, 0, j - 8)))
-        return is_q, t
-
-    def stage(j, q_step, h_step):
-        real = (j >= 0) & (j < 16)
-        is_q, t = unit(j)
-
-        @pl.when(real & is_q)
-        def _():
-            q_step(t)
-
-        @pl.when(real & jnp.logical_not(is_q))
-        def _():
-            h_step(t)
-
+        wait_all(att2_in, att2_send, att2_recv).wait_recv()
+        att_ref[...] = att2_in[...].reshape(512, LANES)
+
+    def look_up(i, table):
+        start, count = jnp.int32(0), jnp.int32(0)
+        for at, (first, size) in table.items():
+            start = jnp.where(i == at, first, start)
+            count = jnp.where(i == at, size, count)
+        return start, count
+
+    def run(i, table, step):
+        start, count = look_up(i, table)
+
+        @pl.loop(0, count)
+        def _(u):
+            step(start + u)
+
+    def project(i, table, step, pack, *more):
+        start, count = look_up(i, table)
+        for size in sorted({size for _, size in table.values()}):
+
+            @pl.when(count == size)
+            def _():
+                step(start, size, *more)
+
+        @pl.loop(0, count)
+        def _(u):
+            pack(start + u, u * 2 * rows)
+
+    first_h = min(H_PROJECT)
     loads[2].wait()
     loads[3].wait()
 
-    @pl.loop(0, 19)
-    def _(j):
-        @pl.when(j == 6)
+    @pl.loop(0, PASSES)
+    def _(i):
+        run(i, GATHER, pass_on)
+        project(i, Q_PROJECT, project_q, pack_q)
+        project(i, H_PROJECT, project_h, pack_h, i == first_h)
+
+        @pl.when(i == first_h)
         def _():
-            loads[4].wait()
-            loads[5].wait()
-
-        stage(j, project_q, project_h)
-
-        @pl.when(j == 0)
-        def _():
-            gather_copy(0).wait_recv()
-            side_copy(1).start()
-            gather_copy(3).start()
-            gather_copy(4).start()
-            gather_copy(1).wait_recv()
-            side_copy(2).start()
-            gather_copy(5).start()
-            gather_copy(2).wait_recv()
-            side_copy(3).start()
-
-        @pl.when(j == 3)
-        def _():
-            gather_copy(4).wait_recv()
-            side_copy(5).start()
-            gather_copy(6).start()
-            gather_copy(3).wait_recv()
-            side_copy(4).start()
-
-        @pl.when(j == 6)
-        def _():
-            gather_copy(5).wait_recv()
-            side_copy(6).start()
-            gather_copy(6).wait_recv()
-            side_copy(7).start()
-
-        stage(j - 1, q_sum.second, h_sum.second)
-        stage(j - 2, q_sum.third, h_sum.third)
-        stage(j - 3, finish_q, finish_h)
-
-        @pl.when(j == 13)
+            loads[4].start()
+            loads[5].start()
+
+        run(i, Q_SECOND, q_sum.second)
+        run(i, Q_THIRD, q_sum.third)
+        run(i, H_SECOND, h_sum.second)
+        run(i, H_THIRD, h_sum.third)
+        run(i, Q_LAST, finish_q)
+        run(i, H_LAST, finish_h)
+
+        @pl.when(i == ATTEND)
         def _():
             attend()
 
-        @pl.when(j == 15)
+        @pl.when(i == SPREAD)
         def _():
             spread_heads()
 
     gather_heads()
 
-    for k in range(7):
-        gather_copy(k).wait_send()
-    for t in range(8):
-        side_copy(t).wait_send()
-
-    @pl.loop(0, 8)
-    def _(t):
-        q_sum.finish(t)
-        h_sum.finish(t)
-        for core in range(2):
-            to, copy = q_copy(t, core)
-
-            @pl.when(to != w)
-            def _():
-                copy.wait_send()
-
-    for s in range(1, 8):
-        att1_copy(s).wait_send()
-    for s in range(1, 16):
-        att2_copy(s).wait_send()
+    for part, sem in ((piece.at[0:7, 0], 0), (piece.at[:, 0], 1)):
+        pltpu.make_async_remote_copy(
+            src_ref=part, dst_ref=part, send_sem=ag_send.at[sem], recv_sem=ag_recv.at[0],
+            device_id=side, device_id_type=MESH,
+        ).wait_send()
+    q_sum.finish()
+    h_sum.finish()
+    wait_all(qin, q_send, q_recv).wait_send()
+    wait_all(att1_in, att1_send, att1_recv).wait_send()
+    wait_all(att2_in, att2_send, att2_recv).wait_send()
+
+
+def turn(att, hid, att_out, hid_out):
+    for i in range(4):
+        cols = slice(i * 128, (i + 1) * 128)
+        att_out[:, cols] = att[cols, :].T[0:96]
+        hid_out[0:128, cols] = hid[cols, 0:128].T
+        hid_out[128:256, cols] = hid[cols, 128:256].T
+        hid_out[256:288, cols] = hid[cols, 256:384].T[0:32]
 
 
 def body(
@@ -582,8 +622,8 @@
     attended, hidden = pl.pallas_call(
         kernel,
         out_shape=(
-            jax.ShapeDtypeStruct((512, 96), BF16),
-            jax.ShapeDtypeStruct((512, 288), BF16),
+            jax.ShapeDtypeStruct((512, LANES), BF16),
+            jax.ShapeDtypeStruct((512, 3 * LANES), BF16),
         ),
         in_specs=[anywhere] * 8 + [pl.BlockSpec(memory_space=pltpu.SMEM)],
         out_specs=(vmem, vmem),
@@ -591,32 +631,32 @@
             pltpu.VMEM((rows, width), BF16),
             pltpu.VMEM((width // LANES, LANES), F32),
             pltpu.VMEM(w_query.shape, BF16),
-            pltpu.VMEM(w_keyvalue.shape, BF16),
+            pltpu.VMEM(w_keyvalue.shape[::-1], BF16),
             pltpu.VMEM(w_gate.shape, BF16),
             pltpu.VMEM(w_up.shape, BF16),
             pltpu.VMEM(key_cache.shape, BF16),
             pltpu.VMEM(value_cache.shape, BF16),
-            dma((8,)),
+            dma((6 + 2 * PARTS,)),
             pltpu.VMEM((UNITS, 2, rows, slab), BF16),
             pltpu.VMEM((rows, slab), BF16),
-            dma((15,)),
+            dma((2,)),
             dma((7,)),
             dma((8,)),
-            pltpu.VMEM((2 * rows, 896), F32),
-            pltpu.VMEM((2 * rows, w_gate.shape[1]), BF16),
-            pltpu.VMEM((2 * rows, w_up.shape[1]), BF16),
+            pltpu.VMEM((4 * rows, 896), F32),
+            pltpu.VMEM((4 * rows, w_gate.shape[1]), BF16),
+            pltpu.VMEM((4 * rows, w_up.shape[1]), BF16),
             pltpu.VMEM((UNITS, 2, 4, 896), F32),
             pltpu.VMEM((16, 4, 896), F32),
-            dma((UNITS, 2)),
-            dma((16,)),
+            dma((1,)),
+            dma((1,)),
             pltpu.VMEM((8, 4, 16, LANES), BF16),
             pltpu.VMEM((8, 4, 16, LANES), BF16),
-            dma((8,)),
-            dma((8,)),
+            dma((1,)),
+            dma((1,)),
             pltpu.VMEM((16, 32, LANES), BF16),
             pltpu.VMEM((16, 32, LANES), BF16),
-            dma((16,)),
-            dma((16,)),
+            dma((1,)),
+            dma((1,)),
         ]
         + sum_scratch(Q_SPLIT, F32)
         + sum_scratch(H_SPLIT, BF16),
@@ -624,10 +664,19 @@
             collective_id=0, has_side_effects=True, vmem_limit_bytes=60 * 1024 * 1024
         ),
     )(
-        layer_input, norm_gain.reshape(width // LANES, LANES), w_query, w_keyvalue, w_gate, w_up,
+        layer_input, norm_gain.reshape(width // LANES, LANES), w_query, w_keyvalue.T, w_gate, w_up,
         key_cache, value_cache, cache_lengths,
     )
-    return attended, hidden
+    attended, hidden = pl.pallas_call(
+        turn,
+        out_shape=(
+            jax.ShapeDtypeStruct((96, 512), BF16),
+            jax.ShapeDtypeStruct((288, 512), BF16),
+        ),
+        in_specs=[vmem, vmem],
+        out_specs=(vmem, vmem),
+    )(attended, hidden)
+    return attended.T, hidden.T
 
 
 def solution(mesh):

time: 96.7 us -> 79.6 us (0.82)
  the two profiles are of different devices: /device:TPU:2 before, /device:TPU:1 now
where the time goes in v2:
time: 79.6 us; the launch traced here: 79.5 us
  Pallas kernels  78.8 us (99%)
    pallas_call x1, Pallas kernels, body(): pl.pallas_call(kernel, out_shape=(jax.ShapeDtypeStruct((512, LANES), BF16...  76.8 us
    pallas_call x1, Pallas kernels, body(): pl.pallas_call(turn, out_shape=(jax.ShapeDtypeStruct((96, 512), BF16), ja...  1.98 us

profile of v2, /device:TPU:1, one launch (start us, length us, event | category | flops | bytes accessed | tf_op | source)
XLA Modules:
  0.0 79.5 jit_solution(11464419163733438564)
XLA Ops:
  0.6 76.8 %shard_map.104 = (bf16[512,128]{1,0:T(8,128)(2,1)}, bf16[512,384]{1,0:T(8,128)(2,1)}) custom-call(bf16[32,18432]{1,0:T(8,128)(2,1)} %x_hbm.1, f32[144,128]{1,0:T(8,128)} %bitcast.5, bf16[2304,768]{1,0:T(8,128)(2,1)} %wq_hbm.1, bf16[32,2304]{1,0:T(8,128)(2,1)} %bitcast.4, bf16[2304,2304]{1,0:T(8,128)(2,1)} %wg_hbm.1, bf16[2304,2304]{1,0:T(8,128)(2,1)} %wu_hbm.1, ...), custom_call_target="tpu_custom_call" | custom-call | tf_op jit(solution)/shard_map/pallas_call | solution.py:622
  77.5 2.0 %shard_map.105 = (bf16[96,512]{1,0:T(8,128)(2,1)}, bf16[288,512]{1,0:T(8,128)(2,1)}) custom-call(bf16[512,128]{1,0:T(8,128)(2,1)} %get-tuple-element.6.att, bf16[512,384]{1,0:T(8,128)(2,1)} %get-tuple-element.7.hid), custom_call_target="tpu_custom_call" | custom-call | tf_op jit(solution)/shard_map/pallas_call | solution.py:670

commit v3 on v2

--- a/solution.py
+++ b/solution.py
@@ -17,35 +17,35 @@
 MESSAGES = 10
 PARTS = 3
 GATHER = {
-    1: (1, 1), 2: (2, 2), 4: (5, 1), 5: (4, 1), 6: (6, 1), 8: (7, 1),
+    1: (1, 3), 4: (5, 1), 5: (4, 1), 6: (6, 1), 7: (7, 1),
 }
 Q_PROJECT = {
-    0: (0, 1), 2: (1, 1), 3: (2, 2), 8: (4, 2), 9: (6, 2),
+    0: (0, 1), 2: (1, 1), 3: (2, 2), 7: (4, 2), 8: (6, 2),
 }
 H_PROJECT = {
-    4: (0, 2), 9: (6, 2), 15: (4, 2), 18: (2, 2),
+    4: (0, 2), 8: (6, 2), 13: (2, 2), 18: (4, 2),
 }
 Q_SECOND = {
-    1: (0, 1), 6: (1, 1), 7: (3, 1), 8: (2, 1), 12: (5, 1), 13: (4, 1), 14: (6, 2),
+    1: (0, 1), 4: (1, 1), 6: (2, 2), 9: (4, 1), 10: (5, 2), 12: (7, 1),
 }
 Q_THIRD = {
-    3: (0, 1), 10: (3, 1), 11: (2, 1), 12: (1, 1), 16: (4, 1), 17: (5, 3),
+    8: (0, 1), 9: (1, 1), 10: (3, 1), 11: (2, 1), 14: (4, 1), 15: (6, 1), 16: (5, 1), 17: (7, 1),
 }
 H_SECOND = {
-    9: (0, 1), 16: (1, 1), 17: (6, 2), 23: (4, 2), 24: (3, 1), 25: (2, 1),
+    10: (0, 1), 15: (1, 1), 17: (6, 1), 19: (3, 1), 20: (2, 1), 21: (7, 1), 23: (5, 1), 25: (4, 1),
 }
 H_THIRD = {
-    23: (6, 1), 25: (7, 1), 26: (0, 1), 27: (4, 2), 28: (3, 1), 29: (1, 1), 30: (2, 1),
+    19: (0, 1), 22: (1, 1), 23: (6, 1), 24: (2, 1), 26: (5, 1), 27: (3, 1), 29: (7, 1), 30: (4, 1),
 }
 Q_LAST = {
-    15: (3, 1), 16: (1, 1), 18: (4, 1), 19: (0, 1), 20: (7, 1), 21: (5, 2), 22: (2, 1),
+    13: (0, 1), 18: (1, 3), 20: (4, 1), 21: (5, 3),
 }
 H_LAST = {
-    30: (6, 2), 31: (0, 1), 32: (4, 2), 33: (3, 1), 34: (1, 2),
-}
-ATTEND = 23
-SPREAD = 29
-PASSES = 35
+    27: (6, 1), 28: (1, 2), 31: (5, 1), 32: (7, 1), 33: (4, 1), 34: (0, 1), 35: (3, 1),
+}
+ATTEND = 25
+SPREAD = 30
+PASSES = 36
 
 
 def sum_scratch(split, dtype):

time: 79.6 us -> 78.2 us (0.982)
  Pallas kernels: 78.8 us -> 77.4 us
    pallas_call x1, Pallas kernels: 76.8 us -> 75.4 us  [body(): pl.pallas_call(kernel, out_shape=(jax.ShapeDtypeStruct((512, LANES), BF16...]
where the time goes in v3:
time: 78.2 us; the launch traced here: 78 us
  Pallas kernels  77.4 us (99%)
    pallas_call x1, Pallas kernels, body(): pl.pallas_call(kernel, out_shape=(jax.ShapeDtypeStruct((512, LANES), BF16...  75.4 us
    pallas_call x1, Pallas kernels, body(): pl.pallas_call(turn, out_shape=(jax.ShapeDtypeStruct((96, 512), BF16), ja...  1.98 us

profile of v3, /device:TPU:1, one launch (start us, length us, event | category | flops | bytes accessed | tf_op | source)
XLA Modules:
  0.0 78.0 jit_solution(13820372417661650847)
XLA Ops:
  0.6 75.4 %shard_map.104 = (bf16[512,128]{1,0:T(8,128)(2,1)}, bf16[512,384]{1,0:T(8,128)(2,1)}) custom-call(bf16[32,18432]{1,0:T(8,128)(2,1)} %x_hbm.1, f32[144,128]{1,0:T(8,128)} %bitcast.5, bf16[2304,768]{1,0:T(8,128)(2,1)} %wq_hbm.1, bf16[32,2304]{1,0:T(8,128)(2,1)} %bitcast.4, bf16[2304,2304]{1,0:T(8,128)(2,1)} %wg_hbm.1, bf16[2304,2304]{1,0:T(8,128)(2,1)} %wu_hbm.1, ...), custom_call_target="tpu_custom_call" | custom-call | tf_op jit(solution)/shard_map/pallas_call | solution.py:622
  76.0 2.0 %shard_map.105 = (bf16[96,512]{1,0:T(8,128)(2,1)}, bf16[288,512]{1,0:T(8,128)(2,1)}) custom-call(bf16[512,128]{1,0:T(8,128)(2,1)} %get-tuple-element.6.att, bf16[512,384]{1,0:T(8,128)(2,1)} %get-tuple-element.7.hid), custom_call_target="tpu_custom_call" | custom-call | tf_op jit(solution)/shard_map/pallas_call | solution.py:670

commit v4 on v3

--- a/solution.py
+++ b/solution.py
@@ -238,8 +238,7 @@
         cols = slice(i * part, (i + 1) * part)
         pairs += [(wg_hbm.at[:, cols], wg.at[:, cols]), (wu_hbm.at[:, cols], wu.at[:, cols])]
     loads = [pltpu.make_async_copy(src, dst, load_sem.at[i]) for i, (src, dst) in enumerate(pairs)]
-    for load in loads[0:4]:
-        load.start()
+    loads[0].start()
 
     barrier = pltpu.get_barrier_semaphore()
     for s in range(1, 16):
@@ -249,10 +248,11 @@
     for other in (pair, pair_up, pair_down):
         pl.semaphore_signal(barrier, inc=1, device_id=other, device_id_type=MESH)
 
+    for load in loads[1:4]:
+        load.start()
+
     loads[0].wait()
     loads[1].wait()
-    for load in loads[6:]:
-        load.start()
     step_cols = 1024
 
     def add_block(i, total):
@@ -320,6 +320,8 @@
     side_copy(0).start()
     for k in (1, 2, 0, 3, 4):
         gather_copy(k).start()
+    for load in loads[6:]:
+        load.start()
 
     count = len(sum_refs) // 2
     q_sum = Summer(Q_SPLIT, F32, sum_refs[:count], (x, z), z_up, z_down, across)

time: 78.2 us -> 78.2 us (level)
  no operation moved by 1% of the time
where the time goes in v4:
time: 78.2 us; the launch traced here: 78 us
  Pallas kernels  77.4 us (99%)
    pallas_call x1, Pallas kernels, body(): pl.pallas_call(kernel, out_shape=(jax.ShapeDtypeStruct((512, LANES), BF16...  75.4 us
    pallas_call x1, Pallas kernels, body(): pl.pallas_call(turn, out_shape=(jax.ShapeDtypeStruct((96, 512), BF16), ja...  1.98 us

profile of v4, /device:TPU:1, one launch (start us, length us, event | category | flops | bytes accessed | tf_op | source)
XLA Modules:
  0.0 78.0 jit_solution(4502304032802203122)
XLA Ops:
  0.6 75.4 %shard_map.104 = (bf16[512,128]{1,0:T(8,128)(2,1)}, bf16[512,384]{1,0:T(8,128)(2,1)}) custom-call(bf16[32,18432]{1,0:T(8,128)(2,1)} %x_hbm.1, f32[144,128]{1,0:T(8,128)} %bitcast.5, bf16[2304,768]{1,0:T(8,128)(2,1)} %wq_hbm.1, bf16[32,2304]{1,0:T(8,128)(2,1)} %bitcast.4, bf16[2304,2304]{1,0:T(8,128)(2,1)} %wg_hbm.1, bf16[2304,2304]{1,0:T(8,128)(2,1)} %wu_hbm.1, ...), custom_call_target="tpu_custom_call" | custom-call | tf_op jit(solution)/shard_map/pallas_call | solution.py:624
  76.0 2.0 %shard_map.105 = (bf16[96,512]{1,0:T(8,128)(2,1)}, bf16[288,512]{1,0:T(8,128)(2,1)}) custom-call(bf16[512,128]{1,0:T(8,128)(2,1)} %get-tuple-element.6.att, bf16[512,384]{1,0:T(8,128)(2,1)} %get-tuple-element.7.hid), custom_call_target="tpu_custom_call" | custom-call | tf_op jit(solution)/shard_map/pallas_call | solution.py:672
